TPU v7x, 128 devices: a whole 4x4x4 slice. The times are simulated.
128 devices in a mesh: box: 4 (over x_hi, core), cone: 32 (over x_lo, y, z).
Axes of the slice: x: 4 (x_hi: 2, x_lo: 2; x = x_hi * 2 + x_lo), y: 4, z: 4, core: 2. Of those that a mesh axis runs over, the one named last changes fastest.
Arguments:
- fine_values: bfloat16 [2, 2097152, 256], P(None, ('box', 'cone')), may hold values from -6 to 6
- present: int32 [262144, 8], P(('box', 'cone')), may hold values 0 or 1
- mask_one: int32 [262144, 16], P(('box', 'cone')), may hold values 0 or 1
- mask_two: int32 [32768, 64], P(('box', 'cone')), may hold values 0 or 1
- mask_top: int32 [4096, 256], replicated, may hold values 0 or 1
- interp_one: bfloat16 [8, 4, 64, 64], replicated, may hold values from -0.25 to 0.25
- interp_two: bfloat16 [8, 4, 64, 64], replicated, may hold values from -0.25 to 0.25
- interp_top: bfloat16 [8, 4, 64, 64], replicated, may hold values from -0.25 to 0.25
- factor_one: float32 [2, 8, 4, 4, 64], replicated, may hold values from -4 to 4
- factor_two: float32 [2, 8, 16, 4, 64], replicated, may hold values from -4 to 4
- factor_top: float32 [2, 8, 64, 4, 64], replicated, may hold values from -4 to 4
- cone_order: int32 [64], replicated, may hold values from 0 to 63, each once
Outputs:
- top_values: float32 [2, 4096, 16384], P(None, None, ('box', 'cone'))
Inputs may be any that keep to these rules, and one draw needn't show every extreme that they name: present and the masks hold 0 or 1. `cone_order`: a permutation of the 64 level-two cones.
All inputs are finite; a program needn't handle non-finite values. No bound on the sum of `present` or of `mask_one` or of `mask_two` on one device may be relied on, other than what follows from the above.
Results may differ from a plain program's by a relative error of at most 0.0064.
Values may be sent and summed in bfloat16 or wider, within the bound.
A program may use at most 256 MiB of HBM per device.

v0:
```python
import jax
import jax.numpy as jnp
from jax import lax
from jax.sharding import PartitionSpec as P

NP = 64
Q0 = 4
Q2 = 64


def kernel(interp, factor):
    weights = interp.astype(jnp.float32)[:, None]
    real_part = factor[0][..., None] * weights
    imag_part = factor[1][..., None] * weights
    stacked = jnp.stack([jnp.stack([real_part, imag_part]), jnp.stack([-imag_part, real_part])])
    return jnp.transpose(stacked, (3, 0, 2, 6, 1, 4, 5)).astype(jnp.bfloat16)


def on_device(
    fine_values,
    present,
    mask_one,
    mask_two,
    mask_top,
    interp_one,
    interp_two,
    interp_top,
    factor_one,
    factor_two,
    factor_top,
    cone_order,
):
    children = fine_values * present.reshape(-1)[None, :, None].astype(jnp.bfloat16)
    boxes_one = children.shape[1] // 8
    blocks_one = children.reshape(2, boxes_one, 8, Q0, NP)
    kernel_one = kernel(interp_one, factor_one)
    result_one = jnp.einsum(
        "rPjcq,crjqzsx->czPsx", blocks_one, kernel_one, preferred_element_type=jnp.float32
    )
    masks_one = jnp.transpose(mask_one.reshape(boxes_one, Q0, 4), (1, 0, 2)).astype(jnp.float32)
    level_one = (result_one * masks_one[:, None, :, :, None]).astype(jnp.bfloat16)
    boxes_two = boxes_one // 8
    blocks_two = level_one.reshape(Q0, 2, boxes_two, 8, 4, NP)
    kernel_two = kernel(interp_two, factor_two).reshape(Q0, 4, 2, 8, NP, 2, 4, NP)
    result_two = jnp.einsum(
        "crPjsq,csrjqzyx->csyzPx", blocks_two, kernel_two, preferred_element_type=jnp.float32
    )
    result_two = result_two.reshape(Q2, 2, boxes_two, NP)
    masks_two = jnp.transpose(mask_two, (1, 0)).astype(jnp.float32)
    level_two = (result_two * masks_two[:, None, :, None]).astype(jnp.bfloat16)
    cone_width = Q2 // lax.axis_size("cone")
    cone_index = lax.axis_index("cone")
    box_index = lax.axis_index("box")
    owned_cones = lax.dynamic_slice_in_dim(cone_order, cone_index * cone_width, cone_width)
    ordered = jnp.take(level_two, cone_order, axis=0)
    relaid = lax.all_to_all(ordered, "cone", split_axis=0, concat_axis=2, tiled=True)
    parents = relaid.shape[2] // 8
    factor_own = jnp.take(factor_top, owned_cones, axis=2)
    factor_sub = lax.dynamic_slice_in_dim(factor_own, box_index, 1, 3)
    interp_sub = lax.dynamic_slice_in_dim(interp_top, box_index, 1, 1)
    kernel_top = kernel(interp_sub, factor_sub)
    mask_cols = jnp.take(mask_top, 4 * owned_cones + box_index, axis=1)
    rows_piece = lax.all_gather(
        relaid.reshape(cone_width, 2, parents, 8 * NP), "box", axis=2, tiled=True
    )
    parent_count = rows_piece.shape[2]
    blocks = rows_piece.reshape(cone_width, 2, parent_count, 8, NP)
    result = jnp.einsum(
        "crPjq,crjqzsx->zPcsx", blocks, kernel_top, preferred_element_type=jnp.float32
    )
    mask_rows = mask_cols.astype(jnp.float32)
    result = result * mask_rows[None, :, :, None, None]
    return result.reshape(2, parent_count, cone_width * NP)


def solution(mesh):
    in_specs = (
        P(None, ("box", "cone"), None),
        P(("box", "cone"), None),
        P(("box", "cone"), None),
        P(("box", "cone"), None),
        P(),
        P(),
        P(),
        P(),
        P(),
        P(),
        P(),
        P(),
    )
    out_specs = P(None, None, ("box", "cone"))
    return jax.shard_map(
        on_device, mesh=mesh, in_specs=in_specs, out_specs=out_specs, check_vma=False
    )
```

profile of v0, /device:TPU:1, one launch (start us, length us, event | category | flops | bytes accessed | tf_op | source)
XLA Modules:
  0.0 449.4 jit_solution(10746451984828902588)
XLA Ops:
  6.5 0.0 copy-start
  6.5 0.0 all-gather.2.cloned.1.call-start
  6.5 0.8 compare_select_fusion.1
  7.3 0.7 compare_and_fusion.1
  8.0 1.1 slice_bitcast_fusion
  9.1 0.9 copy.28
  9.9 0.9 copy.26
  10.8 0.9 convert_element_type.65
  11.8 0.8 convert_element_type.63
  12.6 0.3 copy.34
  12.9 0.5 convert_element_type.64
  13.4 14.5 %broadcast_multiply_fusion = bf16[2,16384,256]{2,1,0:T(8,128)(2,1)} fusion(bf16[2,16384,256]{2,1,0:T(8,128)(2,1)} %param.12, bf16[16384]{0:T(1024)(128)(2,1)S(1)} %convert_element_type.64), kind=kLoop, calls=%fused_computation.23 | loop fusion | flops 8388608 | bytes 33587200 | tf_op jit(solution)/shard_map/mul | solution.py:33
  27.9 0.0 copy-start.2
  27.9 0.0 copy-start.1
  27.9 47.9 %reshape.120 = bf16[2,2048,8,4,64]{4,3,2,1,0:T(4,128)(2,1)} reshape(bf16[2,16384,256]{2,1,0:T(8,128)(2,1)} %broadcast_multiply_fusion) | data formatting | bytes 33554432 | tf_op jit(solution)/shard_map/reshape | solution.py:35
  75.7 0.0 copy-done.2
  75.8 0.0 copy-done.1
  75.8 2.6 multiply_convert_fusion.2
  78.4 2.6 maximum_bitcast_fusion.4
  81.1 36.7 %fusion.3 = bf16[4,2,2048,4,64]{2,4,3,1,0:T(8,128)(2,1)} fusion(f32[4,2048,4]{1,2,0:T(4,128)S(1)} %bitcast.101, bf16[2,2048,8,4,64,1,1]{4,3,2,1,0,6,5:T(4,128)(2,1)} %bitcast.94, bf16[1,2,8,4,4,64,64]{6,5,0,2,4,1,3:T(8,128)(2,1)} %get-tuple-element.12, bf16[1,2,8,4,4,64,64]{6,5,0,2,4,1,3:T(8,128)(2,1)S(1)} %get-tuple-element.11), kind=kOutput, calls=%fused_computation.12 | convolution fusion | flops 8600420352 | bytes 29491200 | tf_op jit(solution)/shard_map/rPjcq,crjqzsx->czPsx/dot_general | solution.py:37
  117.8 15.6 %copy.36 = bf16[4,2,2048,4,64]{4,2,3,1,0:T(8,128)(2,1)} copy(bf16[4,2,2048,4,64]{2,4,3,1,0:T(8,128)(2,1)} %fusion.3) | data formatting | bytes 16777216 | tf_op jit(solution)/shard_map/convert_element_type | solution.py:41
  133.4 12.2 %multiply_convert_fusion = (bf16[1,8,16,4,64,64]{5,4,1,3,0,2:T(8,128)(2,1)S(1)}, bf16[1,8,16,4,64,64]{5,4,1,3,0,2:T(8,128)(2,1)S(1)}, bf16[1,8,16,4,64,64]{5,4,1,3,0,2:T(8,128)(2,1)S(1)}) fusion(f32[8,16,4,64]{3,0,2,1:T(8,128)} %copy.28, f32[8,16,4,64]{3,0,2,1:T(8,128)} %copy.26, bf16[8,4,64,64]{3,2,1,0:T(8,128)(2,1)} %param.18), kind=kLoop, calls=%fused_computation.7 | loop fusion | flops 12582912 | bytes 13107200 | tf_op jit(solution)/shard_map/convert.16
  145.6 11.8 %maximum_bitcast_fusion = (bf16[1,2,8,16,4,64,64]{6,5,0,2,4,1,3:T(8,128)(2,1)}, bf16[1,2,8,16,4,64,64]{6,5,0,2,4,1,3:T(8,128)(2,1)}) fusion(bf16[1,8,16,4,64,64]{5,4,1,3,0,2:T(8,128)(2,1)S(1)} %get-tuple-element.13, bf16[1,8,16,4,64,64]{5,4,1,3,0,2:T(8,128)(2,1)S(1)} %get-tuple-element.18, bf16[1,8,16,4,64,64]{5,4,1,3,0,2:T(8,128)(2,1)S(1)} %get-tuple-element.14), kind=kLoop, calls=%fused_computation.9 | loop fusion | flops 8388608 | bytes 29360128 | tf_op jit(solution)/shard_map/stack | solution.py:15
  157.4 22.7 %pad_maximum_fusion = bf16[2,2,8,16,4,64,64]{6,5,0,2,4,1,3:T(8,128)(2,1)} fusion(bf16[1,2,8,16,4,64,64]{6,5,0,2,4,1,3:T(8,128)(2,1)} %get-tuple-element.10, bf16[1,2,8,16,4,64,64]{6,5,0,2,4,1,3:T(8,128)(2,1)} %get-tuple-element.9), kind=kLoop, calls=%fused_computation.3 | loop fusion | flops 8388608 | bytes 33554432 | tf_op jit(solution)/shard_map/stack | solution.py:15
  180.1 21.9 %fusion.18 = f32[4,4,4,2,256,64]{4,5,2,3,1,0:T(8,128)} fusion(bf16[4,4,2,8,64,2,4,64]{4,7,2,3,6,5,1,0:T(8,128)(2,1)} %bitcast.96, bf16[4,2,256,8,4,64,1,1]{5,3,2,4,1,0,7,6:T(8,128)(2,1)} %bitcast.98), kind=kOutput, calls=%fused_computation.33 | convolution fusion | flops 4294967296 | bytes 33554432 | tf_op jit(solution)/shard_map/crPjsq,csrjqzyx->csyzPx/dot_general | solution.py:45
  202.0 0.0 copy-start.3
  202.0 4.0 copy.38
  206.0 0.0 copy-done.3
  206.1 3.9 fusion.10
  209.9 5.0 %gather_fusion.1 = bf16[64,2,256,64]{2,3,1,0:T(8,128)(2,1)} fusion(bf16[64,2,256,64]{2,3,1,0:T(8,128)(2,1)} %fusion.10, s32[1024]{0:T(1024)S(1)} %pad_clamp_fusion.1), kind=kCustom, calls=%fused_computation.1 | custom fusion | bytes 8388864 | tf_op jit(solution)/shard_map/jit(_take)/gather | solution.py:55
  214.9 2.6 broadcast_select_fusion
  217.5 58.4 %all_to_all.15 = bf16[64,2,256,64]{2,3,1,0:T(8,128)(2,1)} all-to-all(bf16[64,2,256,64]{2,3,1,0:T(8,128)(2,1)S(1)} %broadcast_select_fusion), channel_id=1, replica_groups=mesh['box'=4,'cone'=32] {'cone'}, dimensions={0} | all-to-all | bytes 8388608 | tf_op jit(solution)/shard_map/all_to_all | solution.py:56
  275.9 8.4 %copy.39 = bf16[32,2,2,256,64]{4,3,0,2,1:T(8,128)(2,1)} copy(bf16[32,2,2,256,64]{3,4,2,1,0:T(8,128)(2,1)} %bitcast.97) | data formatting | bytes 8388608 | tf_op jit(solution)/shard_map/all_to_all | solution.py:56
  284.3 11.8 %reshape.123 = bf16[2,2,1024,512]{3,2,1,0:T(8,128)(2,1)} reshape(bf16[2,2,32,256,64]{4,3,2,1,0:T(8,128)(2,1)} %bitcast.95) | data formatting | bytes 8388608 | tf_op jit(solution)/shard_map/reshape | solution.py:64
  296.1 0.0 copy-start.4
  296.1 0.0 all-gather.2.cloned.1.call-update
  296.1 5.6 %copy.42 = s32[4096,256]{0,1:T(8,128)} copy(s32[4096,256]{1,0:T(8,128)} %param.16) | data formatting | bytes 8388608 | tf_op args[4]
  301.8 0.0 copy-done.4
  301.8 0.1 compare_and_fusion.2
  301.9 2.8 gather_fusion.2
  304.6 0.0 copy-done
  304.6 0.6 gather_fusion
  305.3 1.0 bitcast_convert_fusion
  306.2 0.1 fusion.24
  306.3 0.3 multiply_convert_fusion.4
  306.7 0.2 maximum_bitcast_fusion.8
  306.9 0.1 convert_bitcast_fusion.1
  307.0 99.7 %all-gather.2.cloned.1.call-done = bf16[2,2,4096,512]{3,2,1,0:T(8,128)(2,1)} async-done(((bf16[2,2,1024,512]{3,2,1,0:T(8,128)(2,1)}), bf16[2,2,4096,512]{3,2,1,0:T(8,128)(2,1)}) %all-gather.2.cloned.1.call-update) | async-done | bytes 16777232 | tf_op jit(solution)/shard_map/all_gather | solution.py:63
  406.7 20.8 %copy.40 = bf16[2,2,4096,512]{2,3,1,0:T(8,128)(2,1)} copy(bf16[2,2,4096,512]{3,2,1,0:T(8,128)(2,1)} %all-gather.2.cloned.1.call-done) | data formatting | bytes 33554432 | tf_op jit(solution)/shard_map/all_gather | solution.py:63
  427.5 7.1 %fusion.14 = f32[2,4096,2,1,64]{1,4,0,2,3:T(8,128)S(1)} fusion(bf16[2,2,4096,8,64,1]{2,4,3,1,0,5:T(8,128)(2,1)} %bitcast.99, f32[4096,2]{0,1:T(2,128)S(1)} %convert_bitcast_fusion.1, bf16[1,2,8,2,1,64,64]{6,5,0,2,1,3,4:T(8,128)(2,1)S(1)} %get-tuple-element.24, bf16[1,2,8,2,1,64,64]{6,5,0,2,1,3,4:T(8,128)(2,1)S(1)} %get-tuple-element.23), kind=kOutput, calls=%fused_computation.27 | convolution fusion | flops 2148794368 | bytes 21528576 | tf_op jit(solution)/shard_map/crPjq,crjqzsx->zPcsx/dot_general | solution.py:68
  434.6 2.4 copy.43
  437.0 5.6 %copy.44 = f32[2,4096,128]{2,1,0:T(8,128)} copy(f32[2,4096,128]{1,2,0:T(8,128)} %bitcast.100) | data formatting | bytes 8388608 | tf_op jit(solution)/shard_map/reshape | solution.py:73
  (8 shorter events, 0.1 us)
Async XLA Ops:
  6.5 298.1 %copy-start = (f32[2,8,64,4,64]{4,3,2,1,0:T(4,128)S(1)}, f32[2,8,64,4,64]{4,3,2,1,0:T(4,128)}, u32[]{:S(2)}) copy-start(f32[2,8,64,4,64]{4,3,2,1,0:T(4,128)} %param.22) | copy-start | bytes 3145732
  6.5 400.1 %all-gather.2.cloned.1.call-start = ((), (), s32[]{:S(2)}) async-start(), calls=%async_computation.1 | async-start | bytes 20971520 | tf_op jit(solution)/shard_map/all_gather | solution.py:63
  27.9 47.9 %copy-start.2 = (f32[2,8,4,4,64]{4,3,2,1,0:T(4,128)S(1)}, f32[2,8,4,4,64]{4,3,2,1,0:T(4,128)}, u32[]{:S(2)}) copy-start(f32[2,8,4,4,64]{4,3,2,1,0:T(4,128)} %param.20) | copy-start | bytes 196612
  27.9 47.9 %copy-start.1 = (bf16[8,4,64,64]{3,2,1,0:T(8,128)(2,1)S(1)}, bf16[8,4,64,64]{3,2,1,0:T(8,128)(2,1)}, u32[]{:S(2)}) copy-start(bf16[8,4,64,64]{3,2,1,0:T(8,128)(2,1)} %param.17) | copy-start | bytes 786436
  202.0 4.0 copy-start.3
  296.1 5.7 %copy-start.4 = (s32[64]{0:T(128)S(1)}, s32[64]{0:T(128)}, u32[]{:S(2)}) copy-start(s32[64]{0:T(128)} %param.23) | copy-start | bytes 772
Sparse Core Ops, SparseCore 0:
  296.3 110.3 all-gather.1
where the time goes:
time: 453 us; the launch traced here: 449 us
  local copies, waits for them, and re-layouts  134 us (30%)
  waiting for transfers between devices  99.7 us (22%)
  other arithmetic  77.9 us (17%)
  matrix products  65.7 us (15%)
  blocking collectives  58.4 us (13%)
  between operations  13.6 us (3%)
    all_gather x1, waiting for transfers between devices, on_device(): lax.all_gather(relaid.reshape(cone_width, 2, parents, 8 * NP), 'box', axi...  99.7 us
    all_to_all x1, blocking collectives, on_device(): lax.all_to_all(ordered, 'cone', split_axis=0, concat_axis=2, tiled=True)  58.4 us
    reshape x1, local copies, waits for them, and re-layouts, on_device(): blocks_one = children.reshape(2, boxes_one, 8, Q0, NP)  47.9 us
    another operation x4, other arithmetic, kernel(): jnp.stack([jnp.stack([real_part, imag_part]), jnp.stack([-imag_part, real...  37.4 us
    dot_general x1, matrix products, on_device(): jnp.einsum('rPjcq,crjqzsx->czPsx', blocks_one, kernel_one, preferred_elem...  36.7 us
    dot_general x1, matrix products, on_device(): jnp.einsum('crPjsq,csrjqzyx->csyzPx', blocks_two, kernel_two, preferred_e...  21.9 us
    all_gather x1, local copies, waits for them, and re-layouts, on_device(): lax.all_gather(relaid.reshape(cone_width, 2, parents, 8 * NP), 'box', axi...  20.8 us
    convert_element_type x1, local copies, waits for them, and re-layouts, on_device(): (result_one * masks_one[:, None, :, :, None]).astype(jnp.bfloat16)  15.6 us
  transfers between devices with their start and end apart: 1, of which 1 were waited for; matrix products, arithmetic and copies ran while one was open for 2% of the time, Pallas kernels for 0%

commit v1 on v0

v1 whole, which is shorter than its diff:
```python
import functools

import jax
import jax.numpy as jnp
from jax import lax
from jax.experimental import pallas as pl
from jax.experimental.pallas import tpu as pltpu
from jax.sharding import PartitionSpec as P

F32 = jnp.float32
BF16 = jnp.bfloat16
MESH = pl.DeviceIdType.MESH

DEVICES = 128
B1 = 2048
CHUNKS = 4
BLOCK = 256
BLOCKS = B1 // BLOCK
PER_CHUNK = BLOCKS // CHUNKS
QUARTER = BLOCK // 4
N2 = B1 // 8 // CHUNKS
N3 = N2 // 8
ROWS3 = 2 * N3


def offsets():
    every = [
        (x, y, z, core) for x in range(4) for y in range(4) for z in range(4) for core in range(2)
    ][1:]
    hops = lambda o: sum(min(v, 4 - v) for v in o[:3])
    order = sorted(range(127), key=lambda i: (i * 77 + 31) % 127)
    return sorted([every[i] for i in order], key=lambda o: -hops(o))


def target(offset):
    box, cone = lax.axis_index("box"), lax.axis_index("cone")
    x = (box // 2) * 2 + cone // 16
    x = (x + offset[0]) % 4
    y = (cone // 4 + offset[1]) % 4
    z = (cone + offset[2]) % 4
    core = (box + offset[3]) % 2
    return (x // 2) * 2 + core, (x % 2) * 16 + y * 4 + z


def prepare_factor(f_ref, scratch, cones):
    for rj in range(16):
        parts = [f_ref[pl.ds(rj * cones * 4 + s, cones, stride=4), :] for s in range(4)]
        scratch[rj] = jnp.concatenate(parts, axis=1)


def prepare_weights(w_ref, scratch):
    row = lax.broadcasted_iota(jnp.int32, (64, 64), 0)
    column = lax.broadcasted_iota(jnp.int32, (64, 64), 1)
    eye = (row == column).astype(BF16)
    for j in range(8):
        scratch[j] = lax.dot_general(
            eye, w_ref[j], (((1,), (1,)), ((), ())), preferred_element_type=F32
        )


def kernel(
    fine, present, mask_one, mask_two, mask_top, w_one, w_two, w_top, f_one, f_two, f_top, order,
    received,
    fine_buf, split, lhs_a, lhs_b, k_one, out_one, lhs_two, k_two, out_two, lhs_top, w_block,
    present_t, mask_one_t, mask_two_t, mask_rows, mask_top_x, wt, fs_one, fs_two, fs_top,
    top_out, send_buf,
    fine_sem, mask_sem, send_sem, recv_sem, local_sem,
):
    box, cone_index = lax.axis_index("box"), lax.axis_index("cone")
    me = box * 32 + cone_index
    low_lane = lambda rows: lax.broadcasted_iota(jnp.int32, (rows, 128), 1) < 64

    def fetch(block, slot):
        return pltpu.make_async_copy(
            fine.at[:, pl.ds(block * (BLOCK * 8), BLOCK * 8), :], fine_buf.at[slot], fine_sem.at[slot]
        )

    fetch(0, 0).start()
    fetch(1, 1).start()
    rows_copy = pltpu.make_async_copy(mask_top.at[pl.ds(me * 32, 32)], mask_rows, mask_sem)
    rows_copy.start()

    barrier = pltpu.get_barrier_semaphore()
    for offset in offsets():
        pl.semaphore_signal(barrier, inc=1, device_id=target(offset), device_id_type=MESH)

    for i in range(B1 // 256):
        at = pl.ds(i * 256, 256)
        present_t[at, :] = present[:, at].astype(F32).T
        mask_one_t[at, :] = mask_one[:, at].astype(F32).T
    mask_two_t[...] = mask_two[...].astype(F32).T
    prepare_factor(f_one, fs_one, 4)
    prepare_factor(f_two, fs_two, 16)
    prepare_factor(f_top, fs_top, 64)

    prepare_weights(w_one, wt)
    for c in range(4):
        for j in range(8):
            at = (j ^ (c % 2)) * 64
            real = fs_one[j, c : c + 1, :] * wt[j]
            imag = fs_one[8 + j, c : c + 1, :] * wt[j]
            k_one[c, at : at + 64, 0:256] = real.astype(BF16)
            k_one[c, at : at + 64, 256:512] = imag.astype(BF16)
            k_one[c, 512 + at : 576 + at, 0:256] = (-imag).astype(BF16)
            k_one[c, 512 + at : 576 + at, 256:512] = real.astype(BF16)

    prepare_weights(w_two, wt)

    @pl.loop(0, 8)
    def _(pair):
        for odd in range(2):
            c = pair * 2 + odd
            for j in range(8):
                at = (j ^ odd) * 64
                k_two[c, at : at + 64, :] = (fs_two[j, pl.ds(c, 1), :] * wt[j]).astype(BF16)
                k_two[c, 512 + at : 576 + at, :] = (fs_two[8 + j, pl.ds(c, 1), :] * wt[j]).astype(BF16)

    prepare_weights(w_top, wt)
    for j in range(8):
        zero = jnp.zeros((64, 256), BF16)
        w_block[0, j, 0:64, :] = wt[j].astype(BF16)
        w_block[0, j, 64:128, :] = zero
        w_block[1, j, 0:64, :] = zero
        w_block[1, j, 64:128, :] = wt[j].astype(BF16)

    rows_copy.wait()
    for i in range(CHUNKS):
        rows = mask_rows[i * N3 : (i + 1) * N3, :].astype(F32)
        for c in range(64):
            for t in range(2):
                at = 4 * c + 2 * t
                mask_top_x[i * 64 + c, :, t * 128 : t * 128 + 128] = jnp.where(
                    low_lane(N3), rows[:, at : at + 1], rows[:, at + 1 : at + 2]
                )

    def relay(slot, block, quarter, lhs):
        low = low_lane(QUARTER)
        for r in range(2):
            for t in range(2):
                split[r, t] = fine_buf[
                    slot, r, pl.ds(quarter * QUARTER * 8, QUARTER * 8), t * 128 : t * 128 + 128
                ].astype(F32)
        here = present_t[pl.ds(block * BLOCK + quarter * QUARTER, QUARTER), :]
        rows = slice(quarter * QUARTER, quarter * QUARTER + QUARTER)
        for m in range(4):
            first = jnp.broadcast_to(here[:, 2 * m : 2 * m + 1], (QUARTER, 128))
            second = jnp.broadcast_to(here[:, 2 * m + 1 : 2 * m + 2], (QUARTER, 128))
            for r in range(2):
                lanes = slice(r * 512 + m * 128, r * 512 + m * 128 + 128)
                for t in range(2):
                    a = split[r, t, pl.ds(2 * m, QUARTER, stride=8), :] * first
                    b = split[r, t, pl.ds(2 * m + 1, QUARTER, stride=8), :] * second
                    b = pltpu.roll(b, 64, 1)
                    lhs[2 * t, rows, lanes] = jnp.where(low, a, b).astype(BF16)
                    lhs[2 * t + 1, rows, lanes] = jnp.where(low, b, a).astype(BF16)

    fetch(0, 0).wait()
    for quarter in range(4):
        relay(0, 0, quarter, lhs_a)
    pl.semaphore_wait(barrier, DEVICES - 1)

    @pl.loop(0, CHUNKS)
    def _(chunk):
        for k in range(PER_CHUNK):
            block = chunk * PER_CHUNK + k
            now, later = (lhs_a, lhs_b) if k % 2 == 0 else (lhs_b, lhs_a)

            @pl.when(block + 1 < BLOCKS)
            def _():
                fetch(block + 1, (k + 1) % 2).wait()

            @pl.when(block + 2 < BLOCKS)
            def _():
                fetch(block + 2, k % 2).start()

            next_block = (block + 1) % BLOCKS
            low = low_lane(32)
            for c in range(4):
                result = jnp.dot(now[c], k_one[c], preferred_element_type=F32)
                masks = mask_one_t[pl.ds(block * BLOCK, BLOCK), :]
                for t in range(2):
                    at = 4 * c + 2 * t
                    mask = jnp.where(low_lane(BLOCK), masks[:, at : at + 1], masks[:, at + 1 : at + 2])
                    for z in range(2):
                        out_one[z, t] = result[:, z * 256 + t * 128 : z * 256 + t * 128 + 128] * mask
                relay((k + 1) % 2, next_block, c, later)
                for z in range(2):
                    rows = slice(z * N2 + k * 32, z * N2 + k * 32 + 32)
                    other = slice((1 - z) * N2 + k * 32, (1 - z) * N2 + k * 32 + 32)
                    for m in range(4):
                        lanes = slice(m * 128, m * 128 + 128)
                        lanes_other = slice(512 + m * 128, 640 + m * 128)
                        for t in range(2):
                            a = out_one[z, t, pl.ds(2 * m, 32, stride=8), :]
                            b = pltpu.roll(out_one[z, t, pl.ds(2 * m + 1, 32, stride=8), :], 64, 1)
                            even, odd = jnp.where(low, a, b), jnp.where(low, b, a)
                            lhs_two[4 * c + 2 * t, rows, lanes] = even.astype(BF16)
                            lhs_two[4 * c + 2 * t + 1, rows, lanes] = odd.astype(BF16)
                            if z == 1:
                                even, odd = -even, -odd
                            lhs_two[4 * c + 2 * t, other, lanes_other] = even.astype(BF16)
                            lhs_two[4 * c + 2 * t + 1, other, lanes_other] = odd.astype(BF16)

        for c in range(16):
            result = jnp.dot(lhs_two[c], k_two[c], preferred_element_type=F32)
            masks = mask_two_t[pl.ds(chunk * N2, N2), :]
            for t in range(2):
                at = 4 * c + 2 * t
                mask = jnp.where(low_lane(N2), masks[:, at : at + 1], masks[:, at + 1 : at + 2])
                for z in range(2):
                    out_two[c % 2, t, z * N2 : (z + 1) * N2, :] = (
                        result[z * N2 : (z + 1) * N2, t * 128 : t * 128 + 128] * mask
                    )
            for j in range(8):
                for t in range(2):
                    lhs_top[j, c * ROWS3 : (c + 1) * ROWS3, t * 128 : t * 128 + 128] = out_two[
                        c % 2, t, pl.ds(j, ROWS3, stride=8), :
                    ].astype(BF16)

        group = 8

        @pl.loop(0, 4 * (16 // group))
        def _(step):
            s = step % 4
            first = (step // 4) * group
            half = pl.multiple_of((s // 2) * 128, 128)
            real = [None] * group
            imag = [None] * group
            for j in range(8):
                part = jnp.dot(
                    lhs_top[j, pl.ds(pl.multiple_of(first * ROWS3, group * ROWS3), group * ROWS3), pl.ds(half, 128)],
                    w_block[s % 2, j],
                    preferred_element_type=F32,
                )
                for g in range(group):
                    re = part[g * ROWS3 : g * ROWS3 + N3]
                    im = part[g * ROWS3 + N3 : (g + 1) * ROWS3]
                    c = 4 * (first + g) + s
                    f0 = fs_top[j, pl.ds(c, 1), :]
                    f1 = fs_top[8 + j, pl.ds(c, 1), :]
                    new_re = f0 * re - f1 * im
                    new_im = f1 * re + f0 * im
                    real[g] = new_re if j == 0 else real[g] + new_re
                    imag[g] = new_im if j == 0 else imag[g] + new_im
            for g in range(group):
                c = 4 * (first + g) + s
                mask = mask_top_x[chunk * 64 + c]
                top_out[c, 0:N3, :] = real[g] * mask
                top_out[c, N3:ROWS3, :] = imag[g] * mask

        @pl.loop(0, 32)
        def _(i):
            low = low_lane(ROWS3)
            c0, c1 = order[2 * i], order[2 * i + 1]
            for t in range(2):
                a = top_out[c0, :, t * 128 : t * 128 + 128]
                b = top_out[c1, :, t * 128 : t * 128 + 128]
                send_buf[chunk, 2 * t * 32 + i] = jnp.where(low, a, pltpu.roll(b, 64, 1)).astype(BF16)
                send_buf[chunk, (2 * t + 1) * 32 + i] = jnp.where(low, pltpu.roll(a, 64, 1), b).astype(BF16)

        pltpu.make_async_copy(send_buf.at[chunk, me], received.at[chunk, me], local_sem).start()
        for offset in offsets():
            to_box, to_cone = target(offset)
            pltpu.make_async_remote_copy(
                src_ref=send_buf.at[chunk, to_box * 32 + to_cone],
                dst_ref=received.at[chunk, me],
                send_sem=send_sem,
                recv_sem=recv_sem,
                device_id=(to_box, to_cone),
                device_id_type=MESH,
            ).start()

    whole = send_buf.at[:, pl.ds(0, DEVICES - 1)]
    pltpu.make_async_copy(send_buf.at[:, 0], send_buf.at[:, 0], local_sem).wait()
    pltpu.make_async_copy(whole, whole, send_sem).wait()
    pltpu.make_async_copy(whole, whole, recv_sem).wait()


def on_device(
    fine_values, present, mask_one, mask_two, mask_top,
    interp_one, interp_two, interp_top, factor_one, factor_two, factor_top, cone_order,
):
    vmem = pl.BlockSpec(memory_space=pltpu.VMEM)
    hbm = pl.BlockSpec(memory_space=pl.ANY)
    received = pl.pallas_call(
        kernel,
        out_shape=jax.ShapeDtypeStruct((CHUNKS, DEVICES, ROWS3, 128), BF16),
        in_specs=[hbm, vmem, vmem, vmem, hbm] + [vmem] * 6 + [pl.BlockSpec(memory_space=pltpu.SMEM)],
        out_specs=hbm,
        scratch_shapes=[
            pltpu.VMEM((2, 2, BLOCK * 8, 256), BF16),
            pltpu.VMEM((2, 2, QUARTER * 8, 128), F32),
            pltpu.VMEM((4, BLOCK, 1024), BF16),
            pltpu.VMEM((4, BLOCK, 1024), BF16),
            pltpu.VMEM((4, 1024, 512), BF16),
            pltpu.VMEM((2, 2, BLOCK, 128), F32),
            pltpu.VMEM((16, 2 * N2, 1024), BF16),
            pltpu.VMEM((16, 1024, 256), BF16),
            pltpu.VMEM((2, 2, 2 * N2, 128), F32),
            pltpu.VMEM((8, 16 * ROWS3, 256), BF16),
            pltpu.VMEM((2, 8, 128, 256), BF16),
            pltpu.VMEM((B1, 8), F32),
            pltpu.VMEM((B1, 16), F32),
            pltpu.VMEM((B1 // 8, 64), F32),
            pltpu.VMEM((32, 256), jnp.int32),
            pltpu.VMEM((CHUNKS * 64, N3, 256), F32),
            pltpu.VMEM((8, 64, 256), F32),
            pltpu.VMEM((16, 4, 256), F32),
            pltpu.VMEM((16, 16, 256), F32),
            pltpu.VMEM((16, 64, 256), F32),
            pltpu.VMEM((64, ROWS3, 256), F32),
            pltpu.VMEM((CHUNKS, DEVICES, ROWS3, 128), BF16),
            pltpu.SemaphoreType.DMA((2,)),
            pltpu.SemaphoreType.DMA,
            pltpu.SemaphoreType.DMA,
            pltpu.SemaphoreType.DMA,
            pltpu.SemaphoreType.DMA,
        ],
        compiler_params=pltpu.CompilerParams(
            collective_id=0, has_side_effects=True, vmem_limit_bytes=60 << 20
        ),
        name="levels",
    )(
        fine_values,
        present.T,
        mask_one.T,
        mask_two.T,
        mask_top,
        interp_one.reshape(8, 256, 64),
        interp_two.reshape(8, 256, 64),
        interp_top.reshape(8, 256, 64),
        factor_one.reshape(-1, 64),
        factor_two.reshape(-1, 64),
        factor_top.reshape(-1, 64),
        cone_order,
    )
    top = received.reshape(CHUNKS, DEVICES, 2, N3, 128)
    return jnp.transpose(top, (2, 1, 0, 3, 4)).reshape(2, DEVICES * 32, 128).astype(F32)


def solution(mesh):
    split = P(("box", "cone"), None)
    in_specs = (P(None, ("box", "cone"), None), split, split, split) + (P(),) * 8
    return jax.shard_map(
        on_device,
        mesh=mesh,
        in_specs=in_specs,
        out_specs=P(None, None, ("box", "cone")),
        check_vma=False,
    )
```

time: 453 us -> 84.9 us (0.19)
  local copies, waits for them, and re-layouts: 134 us -> 2.61 us
  waiting for transfers between devices: 99.7 us -> 0 us
  Pallas kernels: 0 us -> 80.2 us
  other arithmetic: 77.9 us -> 1.95 us
  matrix products: 65.7 us -> 0 us
  blocking collectives: 58.4 us -> 0 us
  between operations: 13.6 us -> 0.02 us
    all_gather x1 -> x0, waiting for transfers between devices: 99.7 us -> none  [on_device(): lax.all_gather(relaid.reshape(cone_width, 2, parents, 8 * NP), 'box', axi...]
    pallas_call x0 -> x1, Pallas kernels: none -> 80.2 us  [on_device(): pl.pallas_call(kernel, out_shape=jax.ShapeDtypeStruct((CHUNKS, DEVICES, R...]
    dot_general x3 -> x0, matrix products: 65.7 us -> none  [the longest x1 36.7 us: on_device(): jnp.einsum('rPjcq,crjqzsx->czPsx', blocks_one, kernel_one, preferred_elem...]
    reshape x3 -> x0, local copies, waits for them, and re-layouts: 65.2 us -> none  [the longest x1 47.9 us: on_device(): blocks_one = children.reshape(2, boxes_one, 8, Q0, NP)]
    all_to_all x1 -> x0, blocking collectives: 58.4 us -> none  [on_device(): lax.all_to_all(ordered, 'cone', split_axis=0, concat_axis=2, tiled=True)]
    another operation x7 -> x0, other arithmetic: 52.5 us -> none  [the longest x4 37.4 us: kernel(): jnp.stack([jnp.stack([real_part, imag_part]), jnp.stack([-imag_part, real...]
    all_gather x1 -> x0, local copies, waits for them, and re-layouts: 20.8 us -> none  [on_device(): lax.all_gather(relaid.reshape(cone_width, 2, parents, 8 * NP), 'box', axi...]
    mul x2 -> x0, other arithmetic: 15.4 us -> none  [the longest x1 14.5 us: on_device(): fine_values * present.reshape(-1)[None, :, None].astype(jnp.bfloat16)]
  transfers between devices with their start and end apart: 1 -> 0, of which waited for: 1 -> 0; matrix products, arithmetic and copies ran while one was open for 2% -> 0% of each run, Pallas kernels for 0% -> 0%
where the time goes in v1:
time: 84.9 us; the launch traced here: 84.8 us
  Pallas kernels  80.2 us (94%)
  local copies, waits for them, and re-layouts  2.61 us (3%)
  other arithmetic  1.95 us (2%)
    pallas_call x1, Pallas kernels, on_device(): pl.pallas_call(kernel, out_shape=jax.ShapeDtypeStruct((CHUNKS, DEVICES, R...  80.2 us
    convert_element_type x1, local copies, waits for them, and re-layouts, on_device(): jnp.transpose(top, (2, 1, 0, 3, 4)).reshape(2, DEVICES * 32, 128)  2.61 us
    convert_element_type x1, other arithmetic, on_device(): jnp.transpose(top, (2, 1, 0, 3, 4)).reshape(2, DEVICES * 32, 128)  1.95 us

profile of v1, /device:TPU:1, one launch (start us, length us, event | category | flops | bytes accessed | tf_op | source)
XLA Modules:
  0.0 84.8 jit_solution(2363849634215900246)
XLA Ops:
  0.0 80.2 %levels.1 = bf16[4,128,16,128]{3,2,1,0:T(8,128)(2,1)} custom-call(bf16[2,16384,256]{2,1,0:T(8,128)(2,1)} %fine.1, s32[8,2048]{1,0:T(8,128)} %bitcast.22, s32[16,2048]{1,0:T(8,128)} %bitcast.20, s32[64,256]{1,0:T(8,128)} %bitcast.23, s32[4096,256]{1,0:T(8,128)} %mask_top.1, bf16[8,256,64]{2,1,0:T(8,128)(2,1)} %bitcast.16, bf16[8,256,64]{2,1,0:T(8,128)(2,1)} %bitcast.17, ...), custom_call_target="tpu_custom_call" | custom-call | tf_op jit(solution)/shard_map/levels/pallas_call | solution.py:285
  80.2 2.0 %convert_bitcast_fusion = f32[2,128,4,8,128]{4,3,0,1,2:T(8,128)S(1)} fusion(bf16[4,128,16,128]{3,2,1,0:T(8,128)(2,1)} %levels.1), kind=kLoop, calls=%fused_computation | loop fusion | flops 1048576 | bytes 6291456 | tf_op jit(solution)/shard_map/convert_element_type | solution.py:338
  82.2 2.6 %copy.13 = f32[2,128,4,8,128]{4,3,2,1,0:T(8,128)} copy(f32[2,128,4,8,128]{4,3,0,1,2:T(8,128)S(1)} %convert_bitcast_fusion) | data formatting | bytes 8388608 | tf_op jit(solution)/shard_map/convert_element_type | solution.py:338

commit v2 on v1

v2 whole, which is shorter than its diff:
```python
import functools

import jax
import jax.numpy as jnp
from jax import lax
from jax.experimental import pallas as pl
from jax.experimental.pallas import tpu as pltpu
from jax.sharding import PartitionSpec as P

F32 = jnp.float32
BF16 = jnp.bfloat16
MESH = pl.DeviceIdType.MESH

DEVICES = 128
B1 = 2048
CHUNKS = 4
BLOCK = B1 // CHUNKS
N2 = BLOCK // 8
N3 = N2 // 8
ROWS3 = 2 * N3


def offsets():
    every = [
        (x, y, z, core) for x in range(4) for y in range(4) for z in range(4) for core in range(2)
    ][1:]
    hops = lambda o: sum(min(v, 4 - v) for v in o[:3])
    order = sorted(range(127), key=lambda i: (i * 77 + 31) % 127)
    return sorted([every[i] for i in order], key=lambda o: -hops(o))


def prepare_factor(f_ref, scratch, cones):
    for rj in range(16):
        parts = [f_ref[pl.ds(rj * cones * 4 + s, cones, stride=4), :] for s in range(4)]
        scratch[rj] = jnp.concatenate(parts, axis=1)


def prepare_weights(w_ref, scratch):
    row = lax.broadcasted_iota(jnp.int32, (64, 64), 0)
    column = lax.broadcasted_iota(jnp.int32, (64, 64), 1)
    eye = (row == column).astype(BF16)
    for j in range(8):
        scratch[j] = lax.dot_general(
            eye, w_ref[j], (((1,), (1,)), ((), ())), preferred_element_type=F32
        )


def spread(rows, columns, width, first):
    row = lax.broadcasted_iota(jnp.int32, (rows, columns), 0)
    column = lax.broadcasted_iota(jnp.int32, (rows, columns), 1)
    return (row == first + column // width).astype(BF16)


def kernel(
    fine, mask_top, *refs,
):
    small, (order, received), buffers, refs = refs[:9], refs[9:11], refs[11:20], refs[20:]
    present, mask_one, w_one, f_one, mask_two, w_two, f_two, w_top, f_top = buffers
    (
    fine_buf, here, lhs_one, k_one, lhs_two, k_two, lhs_top, w_block, gather,
    present_t, mask_one_t, mask_two_t, spread_present, spread_one, spread_two, spread_top,
    mask_rows, mask_top_x, wt, fs_one, fs_two, fs_top, top_out, send_buf,
    fine_sem, mask_sem, send_sem, recv_sem, local_sem, small_sem,
    ) = refs
    box, cone_index = lax.axis_index("box"), lax.axis_index("cone")
    me = box * 32 + cone_index
    low_lane = lambda rows: lax.broadcasted_iota(jnp.int32, (rows, 128), 1) < 64

    def fetch(chunk, slot):
        part = BLOCK * 8 // 4
        for r in range(2):
            for i in range(4):
                pltpu.make_async_copy(
                    fine.at[r, pl.ds(chunk * (BLOCK * 8) + i * part, part), :],
                    fine_buf.at[slot, r, pl.ds(i * part, part), :],
                    fine_sem.at[slot],
                ).start()

    def fetched(slot):
        pltpu.make_async_copy(fine_buf.at[slot], fine_buf.at[slot], fine_sem.at[slot]).wait()

    fetch(0, 0)
    copies = [pltpu.make_async_copy(a, b, small_sem.at[i]) for i, (a, b) in enumerate(zip(small, buffers))]
    for copy in copies:
        copy.start()
    rows_copy = pltpu.make_async_copy(mask_top.at[pl.ds(me * 32, 32)], mask_rows, mask_sem)
    rows_copy.start()
    fetch(1, 1)

    x, y, z, core = (box // 2) * 2 + cone_index // 16, cone_index // 4 % 4, cone_index % 4, box % 2
    xs = [(x + i) % 4 for i in range(4)]
    to_x = [(v // 2 * 2, v % 2 * 16) for v in xs]
    to_y = [(y + i) % 4 * 4 for i in range(4)]
    to_z = [(z + i) % 4 for i in range(4)]
    to_core = [core, 1 - core]

    def target(offset):
        to_box, to_cone = to_x[offset[0]]
        return to_box + to_core[offset[3]], to_cone + to_y[offset[1]] + to_z[offset[2]]

    barrier = pltpu.get_barrier_semaphore()
    for offset in offsets():
        pl.semaphore_signal(barrier, inc=1, device_id=target(offset), device_id_type=MESH)

    row = lax.broadcasted_iota(jnp.int32, (256, 256), 0)
    column = lax.broadcasted_iota(jnp.int32, (256, 256), 1)
    gather[...] = (column == (row % 8) * 32 + (row // 8) % 4 * 8 + row // 32).astype(BF16)
    row = lax.broadcasted_iota(jnp.int32, (BLOCK, BLOCK), 0)
    column = lax.broadcasted_iota(jnp.int32, (BLOCK, BLOCK), 1)
    reorder_one = (column == (row % 8) * 64 + (row // 8) % 8 * 8 + row // 64).astype(BF16)
    row = lax.broadcasted_iota(jnp.int32, (N2, N2), 0)
    column = lax.broadcasted_iota(jnp.int32, (N2, N2), 1)
    reorder_two = (column == (row % 8) * 8 + row // 8).astype(BF16)
    turned = lambda order, mask: lax.dot_general(
        order, mask.astype(F32).astype(BF16), (((1,), (1,)), ((), ())), preferred_element_type=F32
    ).astype(BF16)
    copies[0].wait()
    copies[1].wait()
    copies[4].wait()
    for i in range(CHUNKS):
        at = slice(i * BLOCK, (i + 1) * BLOCK)
        present_t[at, :] = turned(reorder_one, present[:, at])
        mask_one_t[at, :] = turned(reorder_one, mask_one[:, at])
        at = slice(i * N2, (i + 1) * N2)
        mask_two_t[at, :] = turned(reorder_two, mask_two[:, at])
    spread_present[...] = spread(8, 1024, 128, 0)
    for c in range(4):
        spread_one[c] = spread(16, 256, 64, 4 * c)
    for c in range(16):
        spread_two[c] = spread(64, 256, 64, 4 * c)
    spread_top[...] = spread(16, 1024, 64, 0)
    def relay(slot, chunk):
        low = low_lane(16)
        for half in range(2):
            at = pl.ds(chunk * BLOCK + half * 256, 256)
            here[half] = jnp.dot(present_t[at, :], spread_present[...], preferred_element_type=F32)
            for pair in range(4):
                for r in range(2):
                    picked = []
                    for j2 in (2 * pair, 2 * pair + 1):
                        rows = [
                            fine_buf[slot, r, (8 * p + j2) * 64 + half * 32 : (8 * p + j2) * 64 + half * 32 + 32, :]
                            for p in range(8)
                        ]
                        picked.append(
                            jnp.dot(gather[...], jnp.concatenate(rows, axis=0), preferred_element_type=F32)
                        )
                    for j1 in range(4):
                        at = j1 * 64 + pair * 16
                        to = half * 256 + at
                        for m in range(4):
                            lanes = slice(r * 512 + m * 128, r * 512 + m * 128 + 128)
                            for t in range(2):
                                a, b = [
                                    jnp.concatenate(
                                        [
                                            part[j * 32 + j1 * 8 : j * 32 + j1 * 8 + 8, t * 128 : t * 128 + 128]
                                            for part in picked
                                        ],
                                        axis=0,
                                    )
                                    * here[half, at : at + 16, j * 128 : j * 128 + 128]
                                    for j in (2 * m, 2 * m + 1)
                                ]
                                b = pltpu.roll(b, 64, 1)
                                lhs_one[2 * t, to : to + 16, lanes] = jnp.where(low, a, b).astype(BF16)
                                lhs_one[2 * t + 1, to : to + 16, lanes] = jnp.where(low, b, a).astype(BF16)

    fetched(0)
    relay(0, 0)
    fetch(2, 0)

    for i in (2, 3, 5, 6, 7, 8):
        copies[i].wait()
    prepare_factor(f_one, fs_one, 4)
    prepare_factor(f_two, fs_two, 16)
    prepare_factor(f_top, fs_top, 64)

    prepare_weights(w_one, wt)
    for c in range(4):
        for j in range(8):
            at = (j ^ (c % 2)) * 64
            real = fs_one[j, c : c + 1, :] * wt[j]
            imag = fs_one[8 + j, c : c + 1, :] * wt[j]
            k_one[c, at : at + 64, 0:256] = real.astype(BF16)
            k_one[c, at : at + 64, 256:512] = imag.astype(BF16)
            k_one[c, 512 + at : 576 + at, 0:256] = (-imag).astype(BF16)
            k_one[c, 512 + at : 576 + at, 256:512] = real.astype(BF16)

    prepare_weights(w_two, wt)

    @pl.loop(0, 8)
    def _(pair):
        for odd in range(2):
            c = pair * 2 + odd
            for j in range(8):
                at = (j ^ odd) * 64
                k_two[c, at : at + 64, :] = (fs_two[j, pl.ds(c, 1), :] * wt[j]).astype(BF16)
                k_two[c, 512 + at : 576 + at, :] = (fs_two[8 + j, pl.ds(c, 1), :] * wt[j]).astype(BF16)

    prepare_weights(w_top, wt)
    for j in range(8):
        zero = jnp.zeros((64, 256), BF16)
        w_block[0, j, 0:64, :] = wt[j].astype(BF16)
        w_block[0, j, 64:128, :] = zero
        w_block[1, j, 0:64, :] = zero
        w_block[1, j, 64:128, :] = wt[j].astype(BF16)

    rows_copy.wait()
    rows = mask_rows[...].astype(F32).astype(BF16)
    for c in range(16):
        mask_top_x[c] = jnp.dot(
            rows[:, 16 * c : 16 * c + 16], spread_top[...], preferred_element_type=F32
        )

    @pl.loop(0, CHUNKS)
    def _(chunk):
        low = low_lane(N2)
        for c in range(4):
            result = jnp.dot(lhs_one[c], k_one[c], preferred_element_type=F32)
            masks = jnp.dot(
                mask_one_t[pl.ds(chunk * BLOCK, BLOCK), :], spread_one[c], preferred_element_type=F32
            )
            for z in range(2):
                rows = slice(z * N2, z * N2 + N2)
                other = slice((1 - z) * N2, (1 - z) * N2 + N2)
                for m in range(4):
                    lanes = slice(m * 128, m * 128 + 128)
                    lanes_other = slice(512 + m * 128, 640 + m * 128)
                    for t in range(2):
                        a, b = [
                            result[j * N2 : (j + 1) * N2, z * 256 + t * 128 : z * 256 + t * 128 + 128]
                            * masks[j * N2 : (j + 1) * N2, t * 128 : t * 128 + 128]
                            for j in (2 * m, 2 * m + 1)
                        ]
                        b = pltpu.roll(b, 64, 1)
                        even, odd = jnp.where(low, a, b), jnp.where(low, b, a)
                        lhs_two[4 * c + 2 * t, rows, lanes] = even.astype(BF16)
                        lhs_two[4 * c + 2 * t + 1, rows, lanes] = odd.astype(BF16)
                        if z == 1:
                            even, odd = -even, -odd
                        lhs_two[4 * c + 2 * t, other, lanes_other] = even.astype(BF16)
                        lhs_two[4 * c + 2 * t + 1, other, lanes_other] = odd.astype(BF16)

        for c in range(16):
            result = jnp.dot(lhs_two[c], k_two[c], preferred_element_type=F32)
            masks = jnp.dot(mask_two_t[pl.ds(chunk * N2, N2), :], spread_two[c], preferred_element_type=F32)
            for j in range(8):
                at = slice(j * N3, (j + 1) * N3)
                both = [result[z * N2 + j * N3 : z * N2 + (j + 1) * N3] * masks[at] for z in range(2)]
                lhs_top[j, c * ROWS3 : (c + 1) * ROWS3, :] = jnp.concatenate(both, axis=0).astype(BF16)

        for s in range(4):
            half = (s // 2) * 128
            real = [None] * 16
            imag = [None] * 16
            for j in range(8):
                part = jnp.dot(
                    lhs_top[j, :, half : half + 128], w_block[s % 2, j], preferred_element_type=F32
                )
                for g in range(16):
                    re = part[g * ROWS3 : g * ROWS3 + N3]
                    im = part[g * ROWS3 + N3 : (g + 1) * ROWS3]
                    c = 4 * g + s
                    f0 = fs_top[j, c : c + 1, :]
                    f1 = fs_top[8 + j, c : c + 1, :]
                    new_re = f0 * re - f1 * im
                    new_im = f1 * re + f0 * im
                    real[g] = new_re if j == 0 else real[g] + new_re
                    imag[g] = new_im if j == 0 else imag[g] + new_im
            for g in range(16):
                mask = mask_top_x[g, pl.ds(chunk * N3, N3), s * 256 : s * 256 + 256]
                top_out[4 * g + s, 0] = real[g] * mask
                top_out[4 * g + s, 1] = imag[g] * mask

        for i in range(32):
            low = low_lane(N3)
            c0, c1 = order[2 * i], order[2 * i + 1]
            for z in range(2):
                for t in range(2):
                    a = top_out[c0, z, :, t * 128 : t * 128 + 128]
                    b = top_out[c1, z, :, t * 128 : t * 128 + 128]
                    send_buf[chunk, 2 * t * 32 + i, z] = jnp.where(low, a, pltpu.roll(b, 64, 1)).astype(BF16)
                    send_buf[chunk, (2 * t + 1) * 32 + i, z] = jnp.where(
                        low, pltpu.roll(a, 64, 1), b
                    ).astype(BF16)

        @pl.when(chunk == 0)
        def _():
            pl.semaphore_wait(barrier, DEVICES - 1)

        pltpu.make_async_copy(send_buf.at[chunk, me], received.at[:, me, chunk], local_sem).start()
        for offset in offsets():
            to_box, to_cone = target(offset)
            pltpu.make_async_remote_copy(
                src_ref=send_buf.at[chunk, to_box * 32 + to_cone],
                dst_ref=received.at[:, me, chunk],
                send_sem=send_sem,
                recv_sem=recv_sem,
                device_id=(to_box, to_cone),
                device_id_type=MESH,
            ).start()

        @pl.when(chunk + 1 < CHUNKS)
        def _():
            slot = (chunk + 1) % 2
            fetched(slot)
            relay(slot, chunk + 1)

            @pl.when(chunk + 3 < CHUNKS)
            def _():
                fetch(chunk + 3, slot)

    whole = send_buf.at[:, pl.ds(0, DEVICES - 1)]
    pltpu.make_async_copy(send_buf.at[:, 0], send_buf.at[:, 0], local_sem).wait()
    pltpu.make_async_copy(whole, whole, send_sem).wait()
    pltpu.make_async_copy(whole, whole, recv_sem).wait()


def widen(received, top, narrow, wide, in_sem, out_sem):
    part = 1024
    at = [pl.ds(i * part, part) for i in range(8)]
    copies_in = [pltpu.make_async_copy(received.at[a], narrow.at[a], in_sem.at[i]) for i, a in enumerate(at)]
    copies_out = [pltpu.make_async_copy(wide.at[a], top.at[a], out_sem.at[i]) for i, a in enumerate(at)]
    for copy in copies_in:
        copy.start()
    for i, a in enumerate(at):
        copies_in[i].wait()
        wide[a] = narrow[a].astype(F32)
        copies_out[i].start()
    for copy in copies_out:
        copy.wait()


def on_device(
    fine_values, present, mask_one, mask_two, mask_top,
    interp_one, interp_two, interp_top, factor_one, factor_two, factor_top, cone_order,
):
    hbm = pl.BlockSpec(memory_space=pl.ANY)
    received = pl.pallas_call(
        kernel,
        out_shape=jax.ShapeDtypeStruct((2, DEVICES, CHUNKS, N3, 128), BF16),
        in_specs=[hbm] * 11 + [pl.BlockSpec(memory_space=pltpu.SMEM)],
        out_specs=hbm,
        scratch_shapes=[
            pltpu.VMEM((8, B1), jnp.int32),
            pltpu.VMEM((16, B1), jnp.int32),
            pltpu.VMEM((8, 256, 64), BF16),
            pltpu.VMEM((256, 64), F32),
            pltpu.VMEM((64, B1 // 8), jnp.int32),
            pltpu.VMEM((8, 256, 64), BF16),
            pltpu.VMEM((1024, 64), F32),
            pltpu.VMEM((8, 256, 64), BF16),
            pltpu.VMEM((4096, 64), F32),
            pltpu.VMEM((2, 2, BLOCK * 8, 256), BF16),
            pltpu.VMEM((2, 256, 1024), F32),
            pltpu.VMEM((4, BLOCK, 1024), BF16),
            pltpu.VMEM((4, 1024, 512), BF16),
            pltpu.VMEM((16, 2 * N2, 1024), BF16),
            pltpu.VMEM((16, 1024, 256), BF16),
            pltpu.VMEM((8, 16 * ROWS3, 256), BF16),
            pltpu.VMEM((2, 8, 128, 256), BF16),
            pltpu.VMEM((256, 256), BF16),
            pltpu.VMEM((B1, 8), BF16),
            pltpu.VMEM((B1, 16), BF16),
            pltpu.VMEM((B1 // 8, 64), BF16),
            pltpu.VMEM((8, 1024), BF16),
            pltpu.VMEM((4, 16, 256), BF16),
            pltpu.VMEM((16, 64, 256), BF16),
            pltpu.VMEM((16, 1024), BF16),
            pltpu.VMEM((32, 256), jnp.int32),
            pltpu.VMEM((16, 32, 1024), F32),
            pltpu.VMEM((8, 64, 256), F32),
            pltpu.VMEM((16, 4, 256), F32),
            pltpu.VMEM((16, 16, 256), F32),
            pltpu.VMEM((16, 64, 256), F32),
            pltpu.VMEM((64, 2, N3, 256), F32),
            pltpu.VMEM((CHUNKS, DEVICES, 2, N3, 128), BF16),
            pltpu.SemaphoreType.DMA((2,)),
            pltpu.SemaphoreType.DMA,
            pltpu.SemaphoreType.DMA,
            pltpu.SemaphoreType.DMA,
            pltpu.SemaphoreType.DMA,
            pltpu.SemaphoreType.DMA((9,)),
        ],
        compiler_params=pltpu.CompilerParams(
            collective_id=0, has_side_effects=True, vmem_limit_bytes=60 << 20
        ),
        name="levels",
    )(
        fine_values,
        mask_top,
        present.T,
        mask_one.T,
        interp_one.reshape(8, 256, 64),
        factor_one.reshape(-1, 64),
        mask_two.T,
        interp_two.reshape(8, 256, 64),
        factor_two.reshape(-1, 64),
        interp_top.reshape(8, 256, 64),
        factor_top.reshape(-1, 64),
        cone_order,
    )
    top = pl.pallas_call(
        widen,
        out_shape=jax.ShapeDtypeStruct((8192, 128), F32),
        in_specs=[hbm],
        out_specs=hbm,
        scratch_shapes=[
            pltpu.VMEM((8192, 128), BF16),
            pltpu.VMEM((8192, 128), F32),
            pltpu.SemaphoreType.DMA((8,)),
            pltpu.SemaphoreType.DMA((8,)),
        ],
        compiler_params=pltpu.CompilerParams(vmem_limit_bytes=60 << 20),
        name="widen",
    )(received.reshape(8192, 128))
    return top.reshape(2, DEVICES * 32, 128)


def solution(mesh):
    split = P(("box", "cone"), None)
    in_specs = (P(None, ("box", "cone"), None), split, split, split) + (P(),) * 8
    return jax.shard_map(
        on_device,
        mesh=mesh,
        in_specs=in_specs,
        out_specs=P(None, None, ("box", "cone")),
        check_vma=False,
    )
```

time: 84.9 us -> 59.7 us (0.70)
  Pallas kernels: 80.2 us -> 59.4 us
  local copies, waits for them, and re-layouts: 2.61 us -> 0 us
  other arithmetic: 1.95 us -> 0 us
    pallas_call x1 -> x2, Pallas kernels: 80.2 us -> 59.4 us  [the longest x1 56.3 us: on_device(): pl.pallas_call(kernel, out_shape=jax.ShapeDtypeStruct((2, DEVICES, CHUNKS...]
    convert_element_type x1 -> x0, local copies, waits for them, and re-layouts: 2.61 us -> none  [on_device(): jnp.transpose(top, (2, 1, 0, 3, 4)).reshape(2, DEVICES * 32, 128)]
    convert_element_type x1 -> x0, other arithmetic: 1.95 us -> none  [on_device(): jnp.transpose(top, (2, 1, 0, 3, 4)).reshape(2, DEVICES * 32, 128)]
where the time goes in v2:
time: 59.7 us; the launch traced here: 59.6 us
  Pallas kernels  59.4 us (99%)
    pallas_call x1, Pallas kernels, on_device(): pl.pallas_call(kernel, out_shape=jax.ShapeDtypeStruct((2, DEVICES, CHUNKS...  56.3 us
    pallas_call x1, Pallas kernels, on_device(): pl.pallas_call(widen, out_shape=jax.ShapeDtypeStruct((8192, 128), F32), i...  3.12 us

profile of v2, /device:TPU:1, one launch (start us, length us, event | category | flops | bytes accessed | tf_op | source)
XLA Modules:
  0.0 59.6 jit_solution(5859894485452372166)
XLA Ops:
  0.0 56.3 %levels.1 = bf16[2,128,4,8,128]{4,3,2,1,0:T(8,128)(2,1)} custom-call(bf16[2,16384,256]{2,1,0:T(8,128)(2,1)} %fine.1, s32[4096,256]{1,0:T(8,128)} %mask_top.1, s32[8,2048]{1,0:T(8,128)} %bitcast.19, s32[16,2048]{1,0:T(8,128)} %bitcast.17, bf16[8,256,64]{2,1,0:T(8,128)(2,1)} %bitcast.13, f32[256,64]{1,0:T(8,128)} %bitcast.18, s32[64,256]{1,0:T(8,128)} %bitcast.20, ...), custom_call_target="tpu_custom_call" | custom-call | tf_op jit(solution)/shard_map/levels/pallas_call | solution.py:340
  56.3 3.1 %widen.1 = f32[8192,128]{1,0:T(8,128)} custom-call(bf16[8192,128]{1,0:T(8,128)(2,1)} %bitcast.11), custom_call_target="tpu_custom_call" | custom-call | tf_op jit(solution)/shard_map/widen/pallas_call | solution.py:404

commit v3 on v2

--- a/solution.py
+++ b/solution.py
@@ -27,6 +27,16 @@
     hops = lambda o: sum(min(v, 4 - v) for v in o[:3])
     order = sorted(range(127), key=lambda i: (i * 77 + 31) % 127)
     return sorted([every[i] for i in order], key=lambda o: -hops(o))
+
+
+def target(offset):
+    box, cone = lax.axis_index("box"), lax.axis_index("cone")
+    x = (box // 2) * 2 + cone // 16
+    x = (x + offset[0]) % 4
+    y = (cone // 4 + offset[1]) % 4
+    z = (cone + offset[2]) % 4
+    core = (box + offset[3]) % 2
+    return (x // 2) * 2 + core, (x % 2) * 16 + y * 4 + z
 
 
 def prepare_factor(f_ref, scratch, cones):
@@ -52,16 +62,13 @@
 
 
 def kernel(
-    fine, mask_top, *refs,
-):
-    small, (order, received), buffers, refs = refs[:9], refs[9:11], refs[11:20], refs[20:]
-    present, mask_one, w_one, f_one, mask_two, w_two, f_two, w_top, f_top = buffers
-    (
+    fine, present, mask_one, mask_two, mask_top, w_one, w_two, w_top, f_one, f_two, f_top, order,
+    received,
     fine_buf, here, lhs_one, k_one, lhs_two, k_two, lhs_top, w_block, gather,
     present_t, mask_one_t, mask_two_t, spread_present, spread_one, spread_two, spread_top,
     mask_rows, mask_top_x, wt, fs_one, fs_two, fs_top, top_out, send_buf,
-    fine_sem, mask_sem, send_sem, recv_sem, local_sem, small_sem,
-    ) = refs
+    fine_sem, mask_sem, send_sem, recv_sem, local_sem,
+):
     box, cone_index = lax.axis_index("box"), lax.axis_index("cone")
     me = box * 32 + cone_index
     low_lane = lambda rows: lax.broadcasted_iota(jnp.int32, (rows, 128), 1) < 64
@@ -80,23 +87,9 @@
         pltpu.make_async_copy(fine_buf.at[slot], fine_buf.at[slot], fine_sem.at[slot]).wait()
 
     fetch(0, 0)
-    copies = [pltpu.make_async_copy(a, b, small_sem.at[i]) for i, (a, b) in enumerate(zip(small, buffers))]
-    for copy in copies:
-        copy.start()
+    fetch(1, 1)
     rows_copy = pltpu.make_async_copy(mask_top.at[pl.ds(me * 32, 32)], mask_rows, mask_sem)
     rows_copy.start()
-    fetch(1, 1)
-
-    x, y, z, core = (box // 2) * 2 + cone_index // 16, cone_index // 4 % 4, cone_index % 4, box % 2
-    xs = [(x + i) % 4 for i in range(4)]
-    to_x = [(v // 2 * 2, v % 2 * 16) for v in xs]
-    to_y = [(y + i) % 4 * 4 for i in range(4)]
-    to_z = [(z + i) % 4 for i in range(4)]
-    to_core = [core, 1 - core]
-
-    def target(offset):
-        to_box, to_cone = to_x[offset[0]]
-        return to_box + to_core[offset[3]], to_cone + to_y[offset[1]] + to_z[offset[2]]
 
     barrier = pltpu.get_barrier_semaphore()
     for offset in offsets():
@@ -114,9 +107,6 @@
     turned = lambda order, mask: lax.dot_general(
         order, mask.astype(F32).astype(BF16), (((1,), (1,)), ((), ())), preferred_element_type=F32
     ).astype(BF16)
-    copies[0].wait()
-    copies[1].wait()
-    copies[4].wait()
     for i in range(CHUNKS):
         at = slice(i * BLOCK, (i + 1) * BLOCK)
         present_t[at, :] = turned(reorder_one, present[:, at])
@@ -129,6 +119,47 @@
     for c in range(16):
         spread_two[c] = spread(64, 256, 64, 4 * c)
     spread_top[...] = spread(16, 1024, 64, 0)
+    prepare_factor(f_one, fs_one, 4)
+    prepare_factor(f_two, fs_two, 16)
+    prepare_factor(f_top, fs_top, 64)
+
+    prepare_weights(w_one, wt)
+    for c in range(4):
+        for j in range(8):
+            at = (j ^ (c % 2)) * 64
+            real = fs_one[j, c : c + 1, :] * wt[j]
+            imag = fs_one[8 + j, c : c + 1, :] * wt[j]
+            k_one[c, at : at + 64, 0:256] = real.astype(BF16)
+            k_one[c, at : at + 64, 256:512] = imag.astype(BF16)
+            k_one[c, 512 + at : 576 + at, 0:256] = (-imag).astype(BF16)
+            k_one[c, 512 + at : 576 + at, 256:512] = real.astype(BF16)
+
+    prepare_weights(w_two, wt)
+
+    @pl.loop(0, 8)
+    def _(pair):
+        for odd in range(2):
+            c = pair * 2 + odd
+            for j in range(8):
+                at = (j ^ odd) * 64
+                k_two[c, at : at + 64, :] = (fs_two[j, pl.ds(c, 1), :] * wt[j]).astype(BF16)
+                k_two[c, 512 + at : 576 + at, :] = (fs_two[8 + j, pl.ds(c, 1), :] * wt[j]).astype(BF16)
+
+    prepare_weights(w_top, wt)
+    for j in range(8):
+        zero = jnp.zeros((64, 256), BF16)
+        w_block[0, j, 0:64, :] = wt[j].astype(BF16)
+        w_block[0, j, 64:128, :] = zero
+        w_block[1, j, 0:64, :] = zero
+        w_block[1, j, 64:128, :] = wt[j].astype(BF16)
+
+    rows_copy.wait()
+    rows = mask_rows[...].astype(F32).astype(BF16)
+    for c in range(16):
+        mask_top_x[c] = jnp.dot(
+            rows[:, 16 * c : 16 * c + 16], spread_top[...], preferred_element_type=F32
+        )
+
     def relay(slot, chunk):
         low = low_lane(16)
         for half in range(2):
@@ -166,55 +197,16 @@
                                 lhs_one[2 * t, to : to + 16, lanes] = jnp.where(low, a, b).astype(BF16)
                                 lhs_one[2 * t + 1, to : to + 16, lanes] = jnp.where(low, b, a).astype(BF16)
 
-    fetched(0)
-    relay(0, 0)
-    fetch(2, 0)
-
-    for i in (2, 3, 5, 6, 7, 8):
-        copies[i].wait()
-    prepare_factor(f_one, fs_one, 4)
-    prepare_factor(f_two, fs_two, 16)
-    prepare_factor(f_top, fs_top, 64)
-
-    prepare_weights(w_one, wt)
-    for c in range(4):
-        for j in range(8):
-            at = (j ^ (c % 2)) * 64
-            real = fs_one[j, c : c + 1, :] * wt[j]
-            imag = fs_one[8 + j, c : c + 1, :] * wt[j]
-            k_one[c, at : at + 64, 0:256] = real.astype(BF16)
-            k_one[c, at : at + 64, 256:512] = imag.astype(BF16)
-            k_one[c, 512 + at : 576 + at, 0:256] = (-imag).astype(BF16)
-            k_one[c, 512 + at : 576 + at, 256:512] = real.astype(BF16)
-
-    prepare_weights(w_two, wt)
-
-    @pl.loop(0, 8)
-    def _(pair):
-        for odd in range(2):
-            c = pair * 2 + odd
-            for j in range(8):
-                at = (j ^ odd) * 64
-                k_two[c, at : at + 64, :] = (fs_two[j, pl.ds(c, 1), :] * wt[j]).astype(BF16)
-                k_two[c, 512 + at : 576 + at, :] = (fs_two[8 + j, pl.ds(c, 1), :] * wt[j]).astype(BF16)
-
-    prepare_weights(w_top, wt)
-    for j in range(8):
-        zero = jnp.zeros((64, 256), BF16)
-        w_block[0, j, 0:64, :] = wt[j].astype(BF16)
-        w_block[0, j, 64:128, :] = zero
-        w_block[1, j, 0:64, :] = zero
-        w_block[1, j, 64:128, :] = wt[j].astype(BF16)
-
-    rows_copy.wait()
-    rows = mask_rows[...].astype(F32).astype(BF16)
-    for c in range(16):
-        mask_top_x[c] = jnp.dot(
-            rows[:, 16 * c : 16 * c + 16], spread_top[...], preferred_element_type=F32
-        )
-
     @pl.loop(0, CHUNKS)
     def _(chunk):
+        slot = chunk % 2
+        fetched(slot)
+        relay(slot, chunk)
+
+        @pl.when(chunk + 2 < CHUNKS)
+        def _():
+            fetch(chunk + 2, slot)
+
         low = low_lane(N2)
         for c in range(4):
             result = jnp.dot(lhs_one[c], k_one[c], preferred_element_type=F32)
@@ -273,7 +265,8 @@
                 top_out[4 * g + s, 0] = real[g] * mask
                 top_out[4 * g + s, 1] = imag[g] * mask
 
-        for i in range(32):
+        @pl.loop(0, 32, unroll=32)
+        def _(i):
             low = low_lane(N3)
             c0, c1 = order[2 * i], order[2 * i + 1]
             for z in range(2):
@@ -300,16 +293,6 @@
                 device_id=(to_box, to_cone),
                 device_id_type=MESH,
             ).start()
-
-        @pl.when(chunk + 1 < CHUNKS)
-        def _():
-            slot = (chunk + 1) % 2
-            fetched(slot)
-            relay(slot, chunk + 1)
-
-            @pl.when(chunk + 3 < CHUNKS)
-            def _():
-                fetch(chunk + 3, slot)
 
     whole = send_buf.at[:, pl.ds(0, DEVICES - 1)]
     pltpu.make_async_copy(send_buf.at[:, 0], send_buf.at[:, 0], local_sem).wait()
@@ -336,22 +319,14 @@
     fine_values, present, mask_one, mask_two, mask_top,
     interp_one, interp_two, interp_top, factor_one, factor_two, factor_top, cone_order,
 ):
+    vmem = pl.BlockSpec(memory_space=pltpu.VMEM)
     hbm = pl.BlockSpec(memory_space=pl.ANY)
     received = pl.pallas_call(
         kernel,
         out_shape=jax.ShapeDtypeStruct((2, DEVICES, CHUNKS, N3, 128), BF16),
-        in_specs=[hbm] * 11 + [pl.BlockSpec(memory_space=pltpu.SMEM)],
+        in_specs=[hbm, vmem, vmem, vmem, hbm] + [vmem] * 6 + [pl.BlockSpec(memory_space=pltpu.SMEM)],
         out_specs=hbm,
         scratch_shapes=[
-            pltpu.VMEM((8, B1), jnp.int32),
-            pltpu.VMEM((16, B1), jnp.int32),
-            pltpu.VMEM((8, 256, 64), BF16),
-            pltpu.VMEM((256, 64), F32),
-            pltpu.VMEM((64, B1 // 8), jnp.int32),
-            pltpu.VMEM((8, 256, 64), BF16),
-            pltpu.VMEM((1024, 64), F32),
-            pltpu.VMEM((8, 256, 64), BF16),
-            pltpu.VMEM((4096, 64), F32),
             pltpu.VMEM((2, 2, BLOCK * 8, 256), BF16),
             pltpu.VMEM((2, 256, 1024), F32),
             pltpu.VMEM((4, BLOCK, 1024), BF16),
@@ -381,7 +356,6 @@
             pltpu.SemaphoreType.DMA,
             pltpu.SemaphoreType.DMA,
             pltpu.SemaphoreType.DMA,
-            pltpu.SemaphoreType.DMA((9,)),
         ],
         compiler_params=pltpu.CompilerParams(
             collective_id=0, has_side_effects=True, vmem_limit_bytes=60 << 20
@@ -389,15 +363,15 @@
         name="levels",
     )(
         fine_values,
-        mask_top,
         present.T,
         mask_one.T,
+        mask_two.T,
+        mask_top,
         interp_one.reshape(8, 256, 64),
+        interp_two.reshape(8, 256, 64),
+        interp_top.reshape(8, 256, 64),
         factor_one.reshape(-1, 64),
-        mask_two.T,
-        interp_two.reshape(8, 256, 64),
         factor_two.reshape(-1, 64),
-        interp_top.reshape(8, 256, 64),
         factor_top.reshape(-1, 64),
         cone_order,
     )

time: 59.7 us -> 59.2 us (level)
  no operation moved by 1% of the time
where the time goes in v3:
time: 59.2 us; the launch traced here: 59.1 us
  Pallas kernels  59 us (100%)
    pallas_call x1, Pallas kernels, on_device(): pl.pallas_call(kernel, out_shape=jax.ShapeDtypeStruct((2, DEVICES, CHUNKS...  55.9 us
    pallas_call x1, Pallas kernels, on_device(): pl.pallas_call(widen, out_shape=jax.ShapeDtypeStruct((8192, 128), F32), i...  3.12 us

profile of v3, /device:TPU:1, one launch (start us, length us, event | category | flops | bytes accessed | tf_op | source)
XLA Modules:
  0.0 59.1 jit_solution(14817095745581387772)
XLA Ops:
  0.0 55.9 %levels.1 = bf16[2,128,4,8,128]{4,3,2,1,0:T(8,128)(2,1)} custom-call(bf16[2,16384,256]{2,1,0:T(8,128)(2,1)} %fine.1, s32[8,2048]{1,0:T(8,128)} %bitcast.19, s32[16,2048]{1,0:T(8,128)} %bitcast.17, s32[64,256]{1,0:T(8,128)} %bitcast.20, s32[4096,256]{1,0:T(8,128)} %mask_top.1, bf16[8,256,64]{2,1,0:T(8,128)(2,1)} %bitcast.13, bf16[8,256,64]{2,1,0:T(8,128)(2,1)} %bitcast.14, ...), custom_call_target="tpu_custom_call" | custom-call | tf_op jit(solution)/shard_map/levels/pallas_call | solution.py:324
  55.9 3.1 %widen.1 = f32[8192,128]{1,0:T(8,128)} custom-call(bf16[8192,128]{1,0:T(8,128)(2,1)} %bitcast.11), custom_call_target="tpu_custom_call" | custom-call | tf_op jit(solution)/shard_map/widen/pallas_call | solution.py:378
